TPU v7x, 32 devices: a whole 2x2x4 slice. The times are simulated.
32 devices in a mesh: grp: 2 (over y), ep: 4 (over z), tp: 2 (over x), pp: 2 (over core).
Axes of the slice: x: 2, y: 2, z: 4, core: 2. Of those that a mesh axis runs over, the one named last changes fastest.
Arguments:
- queries: bfloat16 [2048, 8192], P(('grp', 'ep', 'pp'), 'tp'), parts along dimension 0, may hold values from -64 to 64
- suffix_keys: bfloat16 [2048, 512], P(('grp', 'ep', 'pp')), parts along dimension 0, may hold values from -6 to 6
- suffix_values: bfloat16 [2048, 512], P(('grp', 'ep', 'pp')), parts along dimension 0, may hold values from -6 to 6
- prefix_keys: bfloat16 [4096, 512], P(('grp', 'ep', 'pp')), parts along dimension 0, may hold values from -8 to 8
- prefix_values: bfloat16 [4096, 512], P(('grp', 'ep', 'pp')), parts along dimension 0, may hold values from -6 to 6
- prefix_groups: int32 [4096], P(('grp', 'ep', 'pp')), parts along dimension 0, may hold values from 0 to 7, never falling along the last dimension, each value on 1 to 1024 neighbouring positions
- shot_counts: int32 [16], P(('grp', 'ep', 'pp')), parts along dimension 0, may hold values from 1 to 8
- lengths: int32 [16], P(('grp', 'ep', 'pp')), parts along dimension 0, may hold values from 32 to 128
- hidden: bfloat16 [2048, 4096], P(('grp', 'ep', 'pp')), parts along dimension 0, may hold values from -6 to 6
- expert_ids: int32 [2048, 8], P(('grp', 'ep')), parts along dimension 0, may hold values from 0 to 127, all different within a row
- gate_weights: float32 [2048, 8], P(('grp', 'ep')), parts along dimension 0, may hold values from 0.1 to 1
- gate_proj: bfloat16 [4, 4096, 1536], P('ep', 'pp', 'tp'), may hold values from -0.09375 to 0.09375
- up_proj: bfloat16 [4, 4096, 1536], P('ep', 'pp', 'tp'), may hold values from -0.09375 to 0.09375
- down_proj: bfloat16 [4, 1536, 4096], P('ep', 'tp', 'pp'), may hold values from -0.15625 to 0.15625
Outputs:
- context: bfloat16 [2048, 8192], P(('grp', 'ep', 'pp'), 'tp'), parts along dimension 0
- moe_out: bfloat16 [2048, 4096], P(('grp', 'ep'), ('pp', 'tp')), parts along dimension 0
There are 2 independent parts, one for each index of `grp`. A program takes and returns all parts, laid end to end along the dimension named above; an argument that names none is the same for every part. Nothing has to cross between parts.
All inputs are finite; a program needn't handle non-finite values.
Results may differ from a plain program's by a relative error of at most 0.022.
Values may be sent and summed in bfloat16 or wider, within the bound.
A program may use at most 128 MiB of HBM per device.

v0:
```python
import jax
import jax.numpy as jnp
from jax import lax
from jax.sharding import PartitionSpec as P

D = 4096
HEADS = 64
KVH = 4
HD = 128
TOP = 8
SUFFIX = 128
CAP = 12


NEG = -1e30


def online_update(state_now, scores, visible, value_rows):
    run_max, run_sum, run_acc = state_now
    scores = jnp.where(visible, scores, NEG)
    new_max = jnp.maximum(run_max, jnp.max(scores, axis=-1))
    factor = jnp.exp(run_max - new_max)
    weights = jnp.where(visible, jnp.exp(scores - new_max[..., None]), 0.0)
    new_sum = run_sum * factor + jnp.sum(weights, axis=-1)
    update = jnp.einsum(
        "tkgs,skd->tkgd",
        weights.astype(jnp.bfloat16),
        value_rows,
        preferred_element_type=jnp.float32,
    )
    return (new_max, new_sum, run_acc * factor[..., None] + update)


def shards(
    queries,
    suffix_keys,
    suffix_values,
    prefix_keys,
    prefix_values,
    prefix_groups,
    shot_counts,
    lengths,
    hidden,
    expert_ids,
    gate_weights,
    gate_proj,
    up_proj,
    down_proj,
):
    tok_rows = queries.shape[0]
    local_heads = queries.shape[1] // HD
    head_group = HEADS // KVH
    kv_heads = max(1, local_heads // head_group)
    per_kv = min(local_heads, head_group)
    kv_width = kv_heads * HD
    kv_first = lax.axis_index("tp") * local_heads // head_group
    score_scale = HD ** (-0.5)

    def select_heads(block):
        return lax.dynamic_slice_in_dim(block, kv_first * HD, kv_width, 1)

    query_heads = queries.reshape(tok_rows, kv_heads, per_kv, HD)
    question_count = shot_counts.shape[0]
    tok_shots = jnp.broadcast_to(shot_counts[:, None], (question_count, SUFFIX)).reshape(-1)
    tok_length = jnp.broadcast_to(lengths[:, None], (question_count, SUFFIX)).reshape(-1)

    def score_of(key_rows):
        shaped = key_rows.reshape(key_rows.shape[0], kv_heads, HD)
        return (
            jnp.einsum("tkgd,skd->tkgs", query_heads, shaped, preferred_element_type=jnp.float32)
            * score_scale
        )

    initial = (
        jnp.full((tok_rows, kv_heads, per_kv), NEG, jnp.float32),
        jnp.zeros((tok_rows, kv_heads, per_kv), jnp.float32),
        jnp.zeros((tok_rows, kv_heads, per_kv, HD), jnp.float32),
    )
    key_rows = lax.all_gather(select_heads(prefix_keys), ("ep", "pp"), axis=0, tiled=True)
    value_rows = lax.all_gather(select_heads(prefix_values), ("ep", "pp"), axis=0, tiled=True)
    segment_ids = lax.all_gather(prefix_groups, ("ep", "pp"), axis=0, tiled=True)
    visible = (segment_ids[None, :] < tok_shots[:, None])[:, None, None, :]
    state_now = online_update(
        initial, score_of(key_rows), visible, value_rows.reshape(value_rows.shape[0], kv_heads, HD)
    )
    question_of = jnp.arange(tok_rows, dtype=jnp.int32) // SUFFIX
    position = jnp.arange(tok_rows, dtype=jnp.int32) % SUFFIX
    own_seen = (
        (question_of[:, None] == question_of[None, :])
        & (position[None, :] <= position[:, None])
        & (position[None, :] < tok_length[None, :])
    )
    own_values = select_heads(suffix_values)
    run_max, run_sum, run_acc = online_update(
        state_now,
        score_of(select_heads(suffix_keys)),
        own_seen[:, None, None, :],
        own_values.reshape(tok_rows, kv_heads, HD),
    )
    attended = run_acc / run_sum[..., None]
    attended = jnp.where((position < tok_length)[:, None, None, None], attended, 0.0)
    context = attended.reshape(tok_rows, local_heads * HD).astype(jnp.bfloat16)
    ep_size = lax.axis_size("ep")
    pp_size = lax.axis_size("pp")
    tp_size = lax.axis_size("tp")
    pp_index = lax.axis_index("pp")
    routed = expert_ids.reshape(pp_size, tok_rows, TOP)
    gate_share = gate_weights.reshape(pp_size, tok_rows, TOP)
    matches = routed[..., None] == jnp.arange(ep_size, dtype=jnp.int32)
    taken = jnp.sum(matches.astype(jnp.int32), axis=2)
    shares = jnp.sum(jnp.where(matches, gate_share[..., None], 0.0), axis=2)
    slot_index = jnp.cumsum(taken, axis=1) - taken
    served = (taken > 0) & (slot_index < CAP)
    slot_table = served[..., None] & (slot_index[..., None] == jnp.arange(CAP, dtype=jnp.int32))
    own_slots = lax.dynamic_index_in_dim(slot_table, pp_index, 0, keepdims=False)
    rows_in = hidden.reshape(tok_rows, pp_size, D // pp_size)
    outgoing = jnp.einsum(
        "tec,tpd->epcd", own_slots.astype(jnp.bfloat16), rows_in, preferred_element_type=jnp.float32
    ).astype(jnp.bfloat16)
    w_gate = gate_proj[0]
    w_up = up_proj[0]
    w_down = down_proj[0]
    unit_width = w_gate.shape[1]
    half_width = w_gate.shape[0]
    row_block = lax.all_to_all(
        outgoing.reshape(ep_size * pp_size, CAP, half_width),
        ("ep", "pp"),
        split_axis=0,
        concat_axis=0,
        tiled=True,
    )
    gate_part = jnp.einsum("sxd,df->sxf", row_block, w_gate, preferred_element_type=jnp.float32)
    up_part = jnp.einsum("sxd,df->sxf", row_block, w_up, preferred_element_type=jnp.float32)
    gate_full, up_full = (
        lax.psum(gate_part.astype(jnp.bfloat16), "pp").astype(jnp.float32),
        lax.psum(up_part.astype(jnp.bfloat16), "pp").astype(jnp.float32),
    )
    active = (
        (jax.nn.silu(gate_full) * up_full)
        .astype(jnp.bfloat16)
        .reshape(ep_size * pp_size * CAP, unit_width)
    )
    col_width = w_down.shape[1] // tp_size
    result = lax.psum_scatter(
        lax.dot_general(
            w_down, active, (((0,), (1,)), ((), ())), preferred_element_type=jnp.float32
        ).astype(jnp.bfloat16),
        "tp",
        scatter_dimension=0,
        tiled=True,
    )
    expert_out = result.reshape(col_width, ep_size, pp_size, CAP)
    returned = lax.all_to_all(expert_out, "ep", split_axis=1, concat_axis=1, tiled=True)
    weight_table = jnp.where(slot_table, shares[..., None], 0.0)
    combined = jnp.einsum("ptec,xepc->ptx", weight_table, returned.astype(jnp.float32))
    moe_out = combined.reshape(pp_size * tok_rows, col_width).astype(jnp.bfloat16)
    return (context, moe_out)


def solution(mesh):
    placed = (
        P(("grp", "ep", "pp"), "tp"),
        P(("grp", "ep", "pp"), None),
        P(("grp", "ep", "pp"), None),
        P(("grp", "ep", "pp"), None),
        P(("grp", "ep", "pp"), None),
        P(("grp", "ep", "pp")),
        P(("grp", "ep", "pp")),
        P(("grp", "ep", "pp")),
        P(("grp", "ep", "pp"), None),
        P(("grp", "ep"), None),
        P(("grp", "ep"), None),
        P("ep", "pp", "tp"),
        P("ep", "pp", "tp"),
        P("ep", "tp", "pp"),
    )
    return jax.shard_map(
        shards,
        mesh=mesh,
        in_specs=placed,
        out_specs=(P(("grp", "ep", "pp"), "tp"), P(("grp", "ep"), ("pp", "tp"))),
        check_vma=False,
    )
```

profile of v0, /device:TPU:0, one launch (start us, length us, event | category | flops | bytes accessed | tf_op | source)
XLA Modules:
  0.0 152.0 jit_solution(6718076928422719528)
XLA Ops:
  8.1 0.9 convert_reduce_fusion
  9.4 1.5 %convolution_convert_fusion = bf16[4,12,2,2048]{3,1,2,0:T(8,128)(2,1)S(1)} fusion(bf16[16,2,8,2048]{3,2,1,0:T(8,128)(2,1)} %bitcast.126, pred[2,128,4,12]{1,3,2,0:T(8,128)(4,1)S(1)} %fusion.55, s32[]{:T(128)S(6)} %select_n.92), kind=kOutput, calls=%fused_computation.16 | convolution fusion | flops 50528256 | bytes 1449988 | tf_op jit(solution)/shard_map/tec,tpd->epcd/dot_general | solution.py:117
  10.9 21.7 %all_to_all.10 = bf16[8,12,2048]{2,1,0:T(8,128)(2,1)S(1)} all-to-all(bf16[8,12,2048]{2,1,0:T(8,128)(2,1)S(1)} %bitcast.124), channel_id=1, replica_groups=mesh['grp'=2,'ep'=4,'tp'=2,'pp'=2] {'ep','pp'}, dimensions={0} | all-to-all | bytes 786432 | tf_op jit(solution)/shard_map/all_to_all | solution.py:125
  32.7 3.1 %fusion.30 = bf16[8,12,768]{2,1,0:T(8,128)(2,1)} fusion(bf16[8,12,2048]{2,1,0:T(8,128)(2,1)S(1)} %all_to_all.10, bf16[1,2048,768]{2,1,0:T(8,128)(2,1)} %param.25), kind=kOutput, calls=%fused_computation.32 | convolution fusion | flops 302063616 | bytes 3686400 | tf_op jit(solution)/shard_map/sxd,df->sxf/dot_general | solution.py:132
  35.8 1.3 fusion.33
  37.2 17.6 %all-reduce.3.cloned.1.call-done = (bf16[8,12,768]{2,1,0:T(8,128)(2,1)}, bf16[8,12,768]{2,1,0:T(8,128)(2,1)}) async-done(((bf16[8,12,768]{2,1,0:T(8,128)(2,1)}, bf16[8,12,768]{2,1,0:T(8,128)(2,1)}), (bf16[8,12,768]{2,1,0:T(8,128)(2,1)}, bf16[8,12,768]{2,1,0:T(8,128)(2,1)})) %all-reduce.3.cloned.1.call-update) | async-done | bytes 294928 | tf_op jit(solution)/shard_map/psum | solution.py:136
  54.7 1.1 fusion.52
  56.0 1.4 fusion.17
  57.5 0.9 constant_dynamic-slice_fusion.3
  59.2 1.6 %constant_dynamic-slice_fusion.2 = bf16[256,256]{1,0:T(8,128)(2,1)} fusion(bf16[256,512]{1,0:T(8,128)(2,1)} %param.18, s32[]{:T(128)S(6)} %select_n.82), kind=kLoop, calls=%fused_computation.76 | loop fusion | bytes 262148 | tf_op jit(solution)/shard_map/dynamic_slice | solution.py:60
  60.8 12.1 %all-gather = s32[8,1,256]{2,1,0:T(1,128)S(1)} all-gather(s32[1,1,256]{2,1,0:T(1,128)S(1)} %bitcast.136), channel_id=1, replica_groups=mesh['grp'=2,'ep'=4,'tp'=2,'pp'=2] {'ep','pp'}, dimensions={0}, use_global_device_ids=true | all-gather | bytes 9216 | tf_op jit(solution)/shard_map/all_gather | solution.py:81
  73.6 2.4 %copy.115 = bf16[16,8,32,128]{3,2,1,0:T(8,128)(2,1)} copy(bf16[16,8,32,128]{3,1,2,0:T(8,128)(2,1)} %bitcast.127) | data formatting | bytes 2097152
  76.1 0.8 constant_dynamic-slice_fusion
  78.3 3.2 %fusion.24 = (f32[128,2,16]{0,2,1:T(8,128)S(1)}, f32[2,128,128,16]{2,1,3,0:T(8,128)}) fusion(pred[128,128]{0,1:T(8,128)(4,1)S(1)} %and_and_fusion, bf16[128,2,128,1]{0,2,3,1:T(8,128)(2,1)S(1)} %bitcast.132, bf16[128,2,16,128]{3,2,1,0:T(8,128)(2,1)} %bitcast.122), kind=kOutput, calls=%fused_computation.27 | convolution fusion | flops 135786496 | bytes 3244032 | tf_op jit(solution)/shard_map/tkgd,skd->tkgs/dot_general | solution.py:70
  81.5 1.0 reshape.224
  82.4 0.9 copy.97
  83.3 3.5 %all-to-all-start.1 = ((bf16[1024,4,2,12]{0,2,3,1:T(2,128)(2,1)}), bf16[1024,4,2,12]{0,2,3,1:T(2,128)(2,1)S(1)}, u32[]{:S(2)}, u32[]{:S(2)}) async-start(bf16[1024,4,2,12]{0,2,3,1:T(2,128)(2,1)} %copy.97), calls=%async_computation.2 | async-start | bytes 393216 | tf_op jit(solution)/shard_map/all_to_all | solution.py:153
  86.9 16.2 %bitcast_reduce_fusion = (f32[128,2,16]{0,2,1:T(8,128)S(1)}, f32[2,2048,128,16]{2,1,3,0:T(8,128)}) fusion(pred[2048]{0:T(1024)(128)(4,1)S(1)} %reshape.228, bf16[2048,2,128,1]{0,2,3,1:T(8,128)(2,1)} %bitcast.125, bf16[128,2,16,128]{3,2,1,0:T(8,128)(2,1)} %bitcast.123), kind=kOutput, calls=%fused_computation.1 | convolution fusion | flops 2172645376 | bytes 35670016 | tf_op jit(solution)/shard_map/tkgd,skd->tkgs/dot_general | solution.py:70
  103.1 15.5 %fusion.2 = f32[128,2,16]{0,2,1:T(8,128)S(1)} fusion(f32[2,2048,128,16]{2,1,3,0:T(8,128)} %get-tuple-element.22, f32[128,2,16]{0,2,1:T(8,128)S(1)} %get-tuple-element.20, pred[2048]{0:T(1024)(128)(4,1)S(1)} %reshape.228), kind=kLoop, calls=%fused_computation.5 | loop fusion | flops 41938944 | bytes 33589248 | tf_op jit(solution)/shard_map/reduce_sum | solution.py:24
  119.8 2.0 %fusion.36 = f32[2,128,128,16]{2,1,3,0:T(8,128)} fusion(bf16[128,2,128,1]{0,2,3,1:T(8,128)(2,1)S(1)} %bitcast.131, f32[2,128,128,16]{2,1,3,0:T(8,128)S(1)} %copy-done.1, f32[128,2,16]{0,2,1:T(8,128)S(1)} %get-tuple-element.19, pred[128,128]{0,1:T(8,128)(4,1)S(1)} %and_and_fusion), kind=kOutput, calls=%fused_computation.34 | convolution fusion | flops 136839168 | bytes 4292608 | tf_op jit(solution)/shard_map/tkgs,skd->tkgd/dot_general | solution.py:25
  121.8 2.3 %copy.87 = bf16[2048,256]{0,1:T(8,128)(2,1)} copy(bf16[2048,256]{1,0:T(8,128)(2,1)} %all-gather.6.cloned.1.call-done) | data formatting | bytes 2097152 | tf_op jit(solution)/shard_map/all_gather | solution.py:80
  124.1 17.1 %fusion.22 = bf16[128,2,16,128]{0,3,2,1:T(8,128)(2,1)} fusion(f32[2,128,128,16]{2,1,3,0:T(8,128)} %fusion.36, bf16[2048,2,128,1]{0,2,3,1:T(8,128)(2,1)} %bitcast.128, f32[2,2048,128,16]{2,1,3,0:T(8,128)} %get-tuple-element.22, f32[128,2,16]{0,2,1:T(8,128)S(1)} %get-tuple-element.20, pred[2048]{0:T(1024)(128)(4,1)S(1)} %reshape.228, ...), kind=kOutput, calls=%fused_computation.22 | convolution fusion | flops 2192572416 | bytes 37816448 | tf_op jit(solution)/shard_map/tkgs,skd->tkgd/dot_general | solution.py:25
  141.2 2.3 %copy.99 = bf16[128,4096]{1,0:T(8,128)(2,1)} copy(bf16[128,4096]{0,1:T(8,128)(2,1)} %bitcast.129) | data formatting | bytes 2097152
  143.4 1.1 fusion.29
  (50 shorter events, 3.5 us)
Async XLA Ops:
  8.0 47.9 %copy-start = (bf16[1,768,2048]{2,1,0:T(8,128)(2,1)S(1)}, bf16[1,768,2048]{2,1,0:T(8,128)(2,1)}, u32[]{:S(2)}) copy-start(bf16[1,768,2048]{2,1,0:T(8,128)(2,1)} %param.27) | copy-start | bytes 9437188
  8.0 46.7 %all-reduce.3.cloned.1.call-start = ((), (), s32[]{:S(2)}) async-start(), calls=%async_computation.6 | async-start | bytes 786432 | tf_op jit(solution)/shard_map/psum | solution.py:136
  10.9 24.9 %copy-start.2 = (bf16[1,2048,768]{2,1,0:T(8,128)(2,1)S(1)}, bf16[1,2048,768]{2,1,0:T(8,128)(2,1)}, u32[]{:S(2)}) copy-start(bf16[1,2048,768]{2,1,0:T(8,128)(2,1)} %param.26) | copy-start | bytes 9437188
  37.1 23.7 %copy-start.7 = (s32[256]{0:T(256)S(1)}, s32[256]{0:T(256)}, u32[]{:S(2)}) copy-start(s32[256]{0:T(256)} %param.19) | copy-start | bytes 3076
  37.1 44.3 %reduce-scatter.2.cloned.1.call-start = ((), (), s32[]{:S(2)}) async-start(), calls=%async_computation.5 | async-start | bytes 589824 | tf_op jit(solution)/shard_map/reduce_scatter | solution.py:144
  55.9 21.9 %copy-start.3 = (s32[256,8]{0,1:T(8,128)S(1)}, s32[256,8]{0,1:T(8,128)}, u32[]{:S(2)}) copy-start(s32[256,8]{0,1:T(8,128)} %param.23) | copy-start | bytes 24580
  56.0 21.9 %copy-start.6 = (f32[256,8]{0,1:T(8,128)S(1)}, f32[256,8]{0,1:T(8,128)}, u32[]{:S(2)}) copy-start(f32[256,8]{0,1:T(8,128)} %param.24) | copy-start | bytes 24580
  57.4 18.7 %copy-start.4 = (bf16[128,512]{1,0:T(8,128)(2,1)S(1)}, bf16[128,512]{1,0:T(8,128)(2,1)}, u32[]{:S(2)}) copy-start(bf16[128,512]{1,0:T(8,128)(2,1)} %param.16) | copy-start | bytes 393220
  57.4 29.5 %all-gather.4.cloned.1.call-start = ((), (), s32[]{:S(2)}) async-start(), calls=%async_computation.3 | async-start | bytes 1179648 | tf_op jit(solution)/shard_map/all_gather | solution.py:79
  59.2 62.7 %all-gather.6.cloned.1.call-start = ((), (), s32[]{:S(2)}) async-start(), calls=%async_computation.4 | async-start | bytes 1179648 | tf_op jit(solution)/shard_map/all_gather | solution.py:80
  77.7 0.6 copy-start.8
  83.3 60.1 %all-to-all-start.1 = ((bf16[1024,4,2,12]{0,2,3,1:T(2,128)(2,1)}), bf16[1024,4,2,12]{0,2,3,1:T(2,128)(2,1)S(1)}, u32[]{:S(2)}, u32[]{:S(2)}) async-start(bf16[1024,4,2,12]{0,2,3,1:T(2,128)(2,1)} %copy.97), calls=%async_computation.2 | async-start | bytes 393216 | tf_op jit(solution)/shard_map/all_to_all | solution.py:153
  103.1 15.5 %copy-start.1 = (f32[2,128,128,16]{2,1,3,0:T(8,128)S(1)}, f32[2,128,128,16]{2,1,3,0:T(8,128)}, u32[]{:S(2)}) copy-start(f32[2,128,128,16]{2,1,3,0:T(8,128)} %get-tuple-element.24) | copy-start | bytes 6291460
  119.8 4.3 %copy-start.5 = (f32[128,2,16]{0,2,1:T(8,128)S(1)}, f32[128,2,16]{0,2,1:T(8,128)}, u32[]{:S(2)}) copy-start(f32[128,2,16]{0,2,1:T(8,128)} %get-tuple-element.17) | copy-start | bytes 49156
  119.8 4.3 %copy-start.9 = (pred[128]{0:T(512)(128)(4,1)S(1)}, pred[128]{0:T(512)(128)(4,1)}, u32[]{:S(2)}) copy-start(pred[128]{0:T(512)(128)(4,1)} %copy-done.8) | copy-start | bytes 388
Sparse Core Ops, SparseCore 0:
  37.2 17.4 all-reduce.2
  57.6 14.2 reduce-scatter.1
Sparse Core Ops, SparseCore 1:
  59.4 25.1 all-gather.3
  86.1 20.6 all-gather.5
where the time goes:
time: 153 us; the launch traced here: 152 us
  matrix products  46.9 us (31%)
  blocking collectives  33.8 us (22%)
  other arithmetic  19.1 us (12%)
  waiting for transfers between devices  17.7 us (12%)
  between operations  17 us (11%)
  local copies, waits for them, and re-layouts  13.7 us (9%)
  starting transfers between devices  3.71 us (2%)
    all_to_all x1, blocking collectives, shards(): lax.all_to_all(outgoing.reshape(ep_size * pp_size, CAP, half_width), ('ep...  21.7 us
    dot_general x2, matrix products, score_of(): jnp.einsum('tkgd,skd->tkgs', query_heads, shaped, preferred_element_type=...  19.4 us
    dot_general x2, matrix products, online_update(): jnp.einsum('tkgs,skd->tkgd', weights.astype(jnp.bfloat16), value_rows, pr...  19.1 us
    psum x1, waiting for transfers between devices, shards(): lax.psum(up_part.astype(jnp.bfloat16), 'pp').astype(jnp.float32)  17.6 us
    reduce_sum x2, other arithmetic, online_update(): new_sum = run_sum * factor + jnp.sum(weights, axis=-1)  16.1 us
    all_gather x1, blocking collectives, shards(): lax.all_gather(prefix_groups, ('ep', 'pp'), axis=0, tiled=True)  12.1 us
    unnamed x24, local copies, waits for them, and re-layouts  5.92 us
    all_to_all x1, starting transfers between devices, shards(): lax.all_to_all(expert_out, 'ep', split_axis=1, concat_axis=1, tiled=True)  3.55 us
  transfers between devices with their start and end apart: 5, of which 1 were waited for; matrix products, arithmetic and copies ran while one was open for 45% of the time, Pallas kernels for 0%

commit v1 on v0

v1 whole, which is shorter than its diff:
```python
import functools
import math

import jax
import jax.numpy as jnp
from jax import lax
from jax.experimental import pallas as pl
from jax.experimental.pallas import tpu as pltpu
from jax.sharding import PartitionSpec as P

D = 4096
HEADS = 64
KVH = 4
HD = 128
TOP = 8
SUFFIX = 128
CAP = 12
PAD = 16
NEG = -1e30
COEF = HD ** (-0.5) * math.log2(math.e)
UNROLL = 4
NT = (((1,), (1,)), ((), ()))
MESH = pl.DeviceIdType.MESH
F32 = jnp.float32
BF16 = jnp.bfloat16


def aligned(value, unit=128):
    return pl.multiple_of(value, unit)


def wide(column_block, width):
    return jnp.concatenate([column_block] * (width // 128), axis=1)


def kernel(
    ep,
    tp,
    q_ref,
    sk_ref,
    sv_ref,
    pk_ref,
    pv_ref,
    pg_ref,
    shots_ref,
    len_ref,
    hid_ref,
    ids_ref,
    gw_ref,
    wg_hbm,
    wu_hbm,
    wd_hbm,
    ctx_ref,
    moe_ref,
    kv,
    kscr,
    vscr,
    ksuf,
    vsuf,
    sbias,
    m_ref,
    acc_ref,
    wg,
    wu,
    wd,
    whi,
    wlo,
    dsend,
    xbuf,
    gown,
    gsend,
    grecv,
    keep,
    tsend,
    trecv,
    rsend,
    rbuf,
    z_up,
    z_dn,
    z_rv,
    p_sd,
    p_rv,
    d_sd,
    d_rv,
    x_sd,
    x_rv,
    g_sd,
    g_rv,
    t_sd,
    t_rv,
    r_sd,
    r_rv,
    w_sem,
):
    z = lax.axis_index("ep")
    x = lax.axis_index("tp")
    c = lax.axis_index("pp")
    me = z * 2 + c
    other = 1 - c
    rows = pk_ref.shape[0]
    heads = q_ref.shape[1] // HD
    group = HEADS // KVH
    kvh = max(1, heads // group)
    per_kv = min(heads, group)
    kvw = kvh * HD
    units = wg.shape[1]
    half = wg.shape[0]
    part = half // tp
    lanes = whi.shape[2]

    barrier = pltpu.get_barrier_semaphore()
    for o in range(1, 2 * ep):
        j = lax.rem(me + o, 2 * ep)
        pl.semaphore_signal(barrier, inc=1, device_id={"ep": j // 2, "pp": j % 2}, device_id_type=MESH)
    for o in range(1, tp):
        pl.semaphore_signal(barrier, inc=1, device_id={"tp": lax.rem(x + o, tp)}, device_id_type=MESH)

    weight_copies = [
        pltpu.make_async_copy(src.at[0], dst, w_sem.at[i])
        for i, (src, dst) in enumerate(((wg_hbm, wg), (wu_hbm, wu), (wd_hbm, wd)))
    ]
    for copy in weight_copies:
        copy.start()

    first = aligned(x * heads // group * HD)
    kv[z, c, 0:rows, :] = pk_ref[:, pl.ds(first, kvw)]
    kv[z, c, rows : 2 * rows, :] = pv_ref[:, pl.ds(first, kvw)]
    ids_row = pg_ref[...].astype(F32)
    if rows < kvw:
        ids_row = jnp.concatenate([ids_row, jnp.zeros((1, kvw - rows), F32)], axis=1)
    kv[z, c, 2 * rows : 2 * rows + 16, :] = jnp.broadcast_to(ids_row, (16, kvw)).astype(BF16)

    lane = lax.broadcasted_iota(jnp.int32, (SUFFIX, lanes), 1)
    expert_of = lax.shift_right_logical(lane, 4)
    slot_of = lane & (PAD - 1)
    usable = (slot_of < CAP) & (lane < ep * PAD)
    below = (
        lax.broadcasted_iota(jnp.int32, (SUFFIX, SUFFIX), 1)
        < lax.broadcasted_iota(jnp.int32, (SUFFIX, SUFFIX), 0)
    )
    below = jnp.where(below, 1.0, 0.0).astype(BF16)
    tables = []
    for b in range(2):
        taken = jnp.zeros((SUFFIX, lanes), F32)
        share = jnp.zeros((SUFFIX, lanes), F32)
        for k in range(TOP):
            named = ids_ref[b * SUFFIX : (b + 1) * SUFFIX, k : k + 1] == expert_of
            taken = jnp.where(named, 1.0, taken)
            share = share + jnp.where(named, gw_ref[b * SUFFIX : (b + 1) * SUFFIX, k : k + 1], 0.0)
        slot = jnp.dot(below, taken.astype(BF16), preferred_element_type=F32)
        hit = (taken > 0.0) & usable & (slot == slot_of.astype(F32))
        tables.append(jnp.where(hit, 1.0, 0.0))
        weight = jnp.where(hit, share, 0.0)
        high = weight.astype(BF16)
        whi[b] = high
        wlo[b] = (weight - high.astype(F32)).astype(BF16)
    own_table = jnp.where(c == 0, tables[0], tables[1])
    pick = own_table.T.astype(BF16)
    for p in range(2):
        columns = aligned(p * half + x * part)
        chosen = jnp.dot(pick, hid_ref[:, pl.ds(columns, part)], preferred_element_type=F32).astype(BF16)
        for e in range(ep):
            dsend[e * 2 + p] = chosen[e * PAD : (e + 1) * PAD]
    xbuf[x, me] = dsend[me]

    pl.semaphore_wait(barrier, 2 * ep - 1 + tp - 1)

    def dispatch_copy(o):
        j = lax.rem(me + o, 2 * ep)
        return pltpu.make_async_remote_copy(
            src_ref=dsend.at[j],
            dst_ref=xbuf.at[x, me],
            send_sem=d_sd.at[o],
            recv_sem=d_rv.at[o],
            device_id={"ep": j // 2, "pp": j % 2},
            device_id_type=MESH,
        )

    def dispatch_arrival(o):
        j = lax.rem(me + 2 * ep - o, 2 * ep)
        return pltpu.make_async_remote_copy(
            src_ref=dsend.at[j],
            dst_ref=xbuf.at[x, j],
            send_sem=d_sd.at[o],
            recv_sem=d_rv.at[o],
            device_id={"ep": j // 2, "pp": j % 2},
            device_id_type=MESH,
        )

    def up_copy(chunk):
        return pltpu.make_async_remote_copy(
            src_ref=kv.at[chunk, c],
            dst_ref=kv.at[chunk, c],
            send_sem=z_up.at[chunk],
            recv_sem=z_rv.at[chunk],
            device_id={"ep": z + 1},
            device_id_type=MESH,
        )

    def down_copy(chunk):
        return pltpu.make_async_remote_copy(
            src_ref=kv.at[chunk, c],
            dst_ref=kv.at[chunk, c],
            send_sem=z_dn.at[chunk],
            recv_sem=z_rv.at[chunk],
            device_id={"ep": z - 1},
            device_id_type=MESH,
        )

    def pair_copy(chunk, core):
        return pltpu.make_async_remote_copy(
            src_ref=kv.at[chunk, core],
            dst_ref=kv.at[chunk, core],
            send_sem=p_sd.at[chunk],
            recv_sem=p_rv.at[chunk],
            device_id={"pp": other},
            device_id_type=MESH,
        )

    pair_copy(z, c).start()
    for o in range(1, 2 * ep):
        dispatch_copy(o).start()

    @pl.when(z < ep - 1)
    def _():
        up_copy(z).start()

    @pl.when(z > 0)
    def _():
        down_copy(z).start()

    def forward_round(s):
        low = z - s
        high = z + s

        @pl.when(low >= 0)
        def _():
            up_copy(low).wait_recv()

            @pl.when(z < ep - 1)
            def _():
                up_copy(low).start()

            pair_copy(low, c).start()

        @pl.when(high <= ep - 1)
        def _():
            down_copy(high).wait_recv()

            @pl.when(z > 0)
            def _():
                down_copy(high).start()

            pair_copy(high, c).start()

    length = len_ref[0]
    shots = shots_ref[0].astype(F32)
    row_id = lax.broadcasted_iota(jnp.int32, (SUFFIX, SUFFIX), 0)
    col_id = lax.broadcasted_iota(jnp.int32, (SUFFIX, SUFFIX), 1)
    sbias[...] = jnp.where((col_id <= row_id) & (col_id < length), 0.0, NEG)
    for g in range(kvh):
        ksuf[g] = sk_ref[:, pl.ds(aligned(first + g * HD), HD)]
        vsuf[g, :, 0:HD] = sv_ref[:, pl.ds(aligned(first + g * HD), HD)]
        vsuf[g, :, HD:] = jnp.ones((SUFFIX, HD), BF16)
        vscr[g, :, HD:] = jnp.ones((2 * rows, HD), BF16)

    unroll = math.gcd(UNROLL, per_kv)

    def own_keys(g):
        @pl.loop(0, per_kv // unroll)
        def _(i):
            for u in range(unroll):
                h = g * per_kv + i * unroll + u
                query = q_ref[:, pl.ds(aligned(h * HD), HD)]
                s = lax.dot_general(query, ksuf[g], NT, preferred_element_type=F32) + sbias[...]
                top = jnp.broadcast_to(jnp.max(s, axis=1, keepdims=True), (SUFFIX, HD))
                weight = jnp.exp2((s - top) * COEF).astype(BF16)
                m_ref[h] = top
                acc_ref[h] = jnp.dot(weight, vsuf[g], preferred_element_type=F32)

    def load_chunk(chunk):
        for core in range(2):
            for g in range(kvh):
                kscr[g, core * rows : (core + 1) * rows, :] = kv[chunk, core, 0:rows, g * HD : (g + 1) * HD]
                vscr[g, core * rows : (core + 1) * rows, 0:HD] = kv[
                    chunk, core, rows : 2 * rows, g * HD : (g + 1) * HD
                ]
        groups = jnp.concatenate(
            [kv[chunk, core, 2 * rows : 2 * rows + 16, :][0:1, 0:rows].astype(F32) for core in range(2)],
            axis=1,
        )
        return jnp.where(groups < shots, 0.0, NEG)

    def prefix_keys(g, bias, last):
        @pl.loop(0, per_kv // unroll)
        def _(i):
            for u in range(unroll):
                h = g * per_kv + i * unroll + u
                columns = pl.ds(aligned(h * HD), HD)
                s = lax.dot_general(q_ref[:, columns], kscr[g], NT, preferred_element_type=F32) + bias
                before = m_ref[h]
                top = jnp.maximum(before, jnp.max(s, axis=1, keepdims=True))
                weight = jnp.exp2((s - wide(top, 2 * rows)) * COEF).astype(BF16)
                factor = jnp.exp2((before - top) * COEF)
                total = acc_ref[h] * wide(factor, 2 * HD) + jnp.dot(
                    weight, vscr[g], preferred_element_type=F32
                )
                if last:
                    mean = total[:, 0:HD] / total[:, HD:]
                    ctx_ref[:, columns] = jnp.where(row_id < length, mean, 0.0).astype(BF16)
                else:
                    m_ref[h] = top
                    acc_ref[h] = total

    def share_copy(o, block):
        return pltpu.make_async_remote_copy(
            src_ref=xbuf.at[block],
            dst_ref=xbuf.at[block],
            send_sem=x_sd.at[o],
            recv_sem=x_rv.at[o],
            device_id={"tp": lax.rem(x + o, tp)},
            device_id_type=MESH,
        )

    def spread():
        for o in range(1, 2 * ep):
            dispatch_arrival(o).wait_recv()
        for o in range(1, tp):
            share_copy(o, x).start()

    sums_copy = pltpu.make_async_remote_copy(
        src_ref=gsend, dst_ref=grecv, send_sem=g_sd.at[0], recv_sem=g_rv.at[0], device_id={"pp": other}, device_id_type=MESH
    )
    tokens = 2 * ep * PAD
    unit_tile = 256 if units % 256 == 0 else units

    def project():
        for o in range(1, tp):
            share_copy(o, lax.rem(x + tp - o, tp)).wait_recv()
        weight_copies[0].wait()
        weight_copies[1].wait()
        for which, w in enumerate((wg, wu)):
            def tile(at, w=w, which=which):
                total = jnp.zeros((tokens, unit_tile), F32)
                for t in range(tp):
                    total = total + jnp.dot(
                        xbuf[t].reshape(tokens, part),
                        w[t * part : (t + 1) * part, at],
                        preferred_element_type=F32,
                    )
                gown[which, :, at] = total
                gsend[which, :, at] = total.astype(BF16)

            if unit_tile == units:
                tile(slice(None))
            else:
                @pl.loop(0, units // unit_tile)
                def _(i, tile=tile):
                    tile(pl.ds(aligned(i * unit_tile), unit_tile))
        sums_copy.start()

    def partial_copy(o):
        return pltpu.make_async_remote_copy(
            src_ref=tsend.at[o],
            dst_ref=trecv.at[o],
            send_sem=t_sd.at[o],
            recv_sem=t_rv.at[o],
            device_id={"tp": lax.rem(x + o, tp)},
            device_id_type=MESH,
        )

    def contract():
        weight_copies[2].wait()
        sums_copy.wait_recv()
        gate = gown[0] + grecv[0].astype(F32)
        up = gown[1] + grecv[1].astype(F32)
        active = (gate / (1.0 + jnp.exp(-gate)) * up).astype(BF16)
        for o in list(range(1, tp)) + [0]:
            base = lax.rem(x + o, tp) * part
            for i in range(part // 256):
                result = jnp.dot(
                    active, wd[:, pl.ds(aligned(base + i * 256), 256)], preferred_element_type=F32
                )
                if o == 0:
                    keep[:, i * 256 : (i + 1) * 256] = result
                else:
                    tsend[o, :, i * 256 : (i + 1) * 256] = result.astype(BF16)
            if o > 0:
                partial_copy(o).start()

    def return_copy(o):
        return pltpu.make_async_remote_copy(
            src_ref=rsend.at[lax.rem(z + o, ep)],
            dst_ref=rbuf.at[z],
            send_sem=r_sd.at[o],
            recv_sem=r_rv.at[o],
            device_id={"ep": lax.rem(z + o, ep)},
            device_id_type=MESH,
        )

    def return_arrival(o):
        source = lax.rem(z + ep - o, ep)
        return pltpu.make_async_remote_copy(
            src_ref=rsend.at[source],
            dst_ref=rbuf.at[source],
            send_sem=r_sd.at[o],
            recv_sem=r_rv.at[o],
            device_id={"ep": source},
            device_id_type=MESH,
        )

    def give_back():
        total = keep[...]
        for o in range(1, tp):
            partial_copy(o).wait_recv()
            total = total + trecv[o].astype(F32)
        rsend[...] = total.astype(BF16).reshape(ep, 2 * PAD, part)
        for o in range(1, ep):
            return_copy(o).start()
        rbuf[z] = rsend[z]

    def combine():
        for o in range(1, ep):
            return_arrival(o).wait_recv()
        for b in range(2):
            served = rbuf[:, b * PAD : (b + 1) * PAD, :].reshape(ep * PAD, part)
            high = whi[b][:, 0 : ep * PAD]
            low = wlo[b][:, 0 : ep * PAD]
            moe_ref[b * SUFFIX : (b + 1) * SUFFIX, :] = (
                jnp.dot(high, served, preferred_element_type=F32)
                + jnp.dot(low, served, preferred_element_type=F32)
            ).astype(BF16)

    phases = [spread, project, contract, give_back, combine]

    for g in range(kvh):
        own_keys(g)

    near = jnp.minimum(z, ep - 1 - z)
    far_sign = jnp.where(z < ep - 1 - z, 1, -1)
    for k in range(ep):
        if k == 0:
            chunk = z
        else:
            forward_round(k)
            both = z + (-1 if k % 2 == 1 else 1) * ((k + 1) // 2)
            chunk = jnp.where(k <= 2 * near, both, z + far_sign * (k - near))
        pair_copy(chunk, other).wait_recv()
        bias = load_chunk(chunk)
        for g in range(kvh):
            prefix_keys(g, bias, k == ep - 1)
            if k == 3 and g == 0 and phases and phases[0] is give_back:
                phases.pop(0)()
        if k < 3 and len(phases) > 2:
            phases.pop(0)()
    while phases:
        phases.pop(0)()

    for o in range(1, 2 * ep):
        dispatch_copy(o).wait_send()
    for o in range(1, tp):
        share_copy(o, x).wait_send()
        partial_copy(o).wait_send()
    for o in range(1, ep):
        return_copy(o).wait_send()
    sums_copy.wait_send()
    for s in range(ep):
        low = z - s
        high = z + s

        @pl.when((low >= 0) & (z < ep - 1))
        def _(low=low):
            up_copy(low).wait_send()

        @pl.when((high <= ep - 1) & (z > 0))
        def _(high=high):
            down_copy(high).wait_send()

        pair_copy(s, c).wait_send()


def shards(ep, tp, queries, suffix_keys, suffix_values, prefix_keys, prefix_values, prefix_groups, shot_counts, lengths, hidden, expert_ids, gate_weights, gate_proj, up_proj, down_proj):
    tok_rows, q_width = queries.shape
    rows = prefix_keys.shape[0]
    heads = q_width // HD
    kvh = max(1, heads // (HEADS // KVH))
    kvw = kvh * HD
    half, units = gate_proj.shape[1:]
    part = half // tp
    lanes = -(-ep * PAD // 128) * 128
    tokens = 2 * ep * PAD
    assert tok_rows == SUFFIX and rows <= kvw
    vmem = pl.BlockSpec(memory_space=pltpu.VMEM)
    smem = pl.BlockSpec(memory_space=pltpu.SMEM)
    hbm = pl.BlockSpec(memory_space=pl.ANY)
    dma = pltpu.SemaphoreType.DMA
    return pl.pallas_call(
        functools.partial(kernel, ep, tp),
        out_shape=(
            jax.ShapeDtypeStruct((tok_rows, q_width), BF16),
            jax.ShapeDtypeStruct((2 * tok_rows, part), BF16),
        ),
        in_specs=[vmem] * 6 + [smem] * 2 + [vmem] * 3 + [hbm] * 3,
        out_specs=(vmem, vmem),
        scratch_shapes=[
            pltpu.VMEM((ep, 2, 2 * rows + 16, kvw), BF16),
            pltpu.VMEM((kvh, 2 * rows, HD), BF16),
            pltpu.VMEM((kvh, 2 * rows, 2 * HD), BF16),
            pltpu.VMEM((kvh, SUFFIX, HD), BF16),
            pltpu.VMEM((kvh, SUFFIX, 2 * HD), BF16),
            pltpu.VMEM((SUFFIX, SUFFIX), F32),
            pltpu.VMEM((heads, SUFFIX, HD), F32),
            pltpu.VMEM((heads, SUFFIX, 2 * HD), F32),
            pltpu.VMEM((half, units), BF16),
            pltpu.VMEM((half, units), BF16),
            pltpu.VMEM((units, half), BF16),
            pltpu.VMEM((2, SUFFIX, lanes), BF16),
            pltpu.VMEM((2, SUFFIX, lanes), BF16),
            pltpu.VMEM((2 * ep, PAD, part), BF16),
            pltpu.VMEM((tp, 2 * ep, PAD, part), BF16),
            pltpu.VMEM((2, tokens, units), F32),
            pltpu.VMEM((2, tokens, units), BF16),
            pltpu.VMEM((2, tokens, units), BF16),
            pltpu.VMEM((tokens, part), F32),
            pltpu.VMEM((tp, tokens, part), BF16),
            pltpu.VMEM((tp, tokens, part), BF16),
            pltpu.VMEM((ep, 2 * PAD, part), BF16),
            pltpu.VMEM((ep, 2 * PAD, part), BF16),
            dma((ep,)),
            dma((ep,)),
            dma((ep,)),
            dma((ep,)),
            dma((ep,)),
            dma((2 * ep,)),
            dma((2 * ep,)),
            dma((tp,)),
            dma((tp,)),
            dma((1,)),
            dma((1,)),
            dma((tp,)),
            dma((tp,)),
            dma((ep,)),
            dma((ep,)),
            dma((3,)),
        ],
        compiler_params=pltpu.CompilerParams(
            collective_id=0, has_side_effects=True, vmem_limit_bytes=50 * 1024 * 1024
        ),
    )(
        queries,
        suffix_keys,
        suffix_values,
        prefix_keys,
        prefix_values,
        prefix_groups.reshape(1, rows),
        shot_counts,
        lengths,
        hidden,
        expert_ids,
        gate_weights,
        gate_proj,
        up_proj,
        down_proj,
    )


def solution(mesh):
    rows = P(("grp", "ep", "pp"), None)
    vector = P(("grp", "ep", "pp"))
    assert mesh.shape["pp"] == 2
    return jax.shard_map(
        functools.partial(shards, mesh.shape["ep"], mesh.shape["tp"]),
        mesh=mesh,
        in_specs=(
            P(("grp", "ep", "pp"), "tp"),
            rows,
            rows,
            rows,
            rows,
            vector,
            vector,
            vector,
            rows,
            P(("grp", "ep"), None),
            P(("grp", "ep"), None),
            P("ep", "pp", "tp"),
            P("ep", "pp", "tp"),
            P("ep", "tp", "pp"),
        ),
        out_specs=(P(("grp", "ep", "pp"), "tp"), P(("grp", "ep"), ("pp", "tp"))),
        check_vma=False,
    )
```

time: 153 us -> 62.1 us (0.41)
  Pallas kernels: 0 us -> 50.8 us
  matrix products: 46.9 us -> 0 us
  blocking collectives: 33.8 us -> 0 us
  other arithmetic: 19.1 us -> 0 us
  waiting for transfers between devices: 17.7 us -> 0 us
  between operations: 17 us -> 1.96 us
  local copies, waits for them, and re-layouts: 13.7 us -> 9.01 us
  starting transfers between devices: 3.71 us -> 0 us
    pallas_call x0 -> x1, Pallas kernels: none -> 50.8 us  [shards(): pl.pallas_call(functools.partial(kernel, ep, tp), out_shape=(jax.ShapeDty...]
    dot_general x9 -> x0, matrix products: 46.9 us -> none  [the longest x2 19.4 us: score_of(): jnp.einsum('tkgd,skd->tkgs', query_heads, shaped, preferred_element_type=...]
    all_to_all x1 -> x0, blocking collectives: 21.7 us -> none  [shards(): lax.all_to_all(outgoing.reshape(ep_size * pp_size, CAP, half_width), ('ep...]
    psum x1 -> x0, waiting for transfers between devices: 17.6 us -> none  [shards(): lax.psum(up_part.astype(jnp.bfloat16), 'pp').astype(jnp.float32)]
    reduce_sum x4 -> x0, other arithmetic: 16.9 us -> none  [the longest x2 16.1 us: online_update(): new_sum = run_sum * factor + jnp.sum(weights, axis=-1)]
    all_gather x1 -> x0, blocking collectives: 12.1 us -> none  [shards(): lax.all_gather(prefix_groups, ('ep', 'pp'), axis=0, tiled=True)]
    all_to_all x1 -> x0, starting transfers between devices: 3.55 us -> none  [shards(): lax.all_to_all(expert_out, 'ep', split_axis=1, concat_axis=1, tiled=True)]
    dynamic_slice x4 -> x0, local copies, waits for them, and re-layouts: 3.45 us -> none  [select_heads(): return lax.dynamic_slice_in_dim(block, kv_first * HD, kv_width, 1)]
  transfers between devices with their start and end apart: 5 -> 0, of which waited for: 1 -> 0; matrix products, arithmetic and copies ran while one was open for 45% -> 0% of each run, Pallas kernels for 0% -> 0%
where the time goes in v1:
time: 62.1 us; the launch traced here: 61.7 us
  Pallas kernels  50.8 us (82%)
  local copies, waits for them, and re-layouts  9.01 us (15%)
  between operations  1.96 us (3%)
    pallas_call x1, Pallas kernels, shards(): pl.pallas_call(functools.partial(kernel, ep, tp), out_shape=(jax.ShapeDty...  50.8 us
    unnamed x16, local copies, waits for them, and re-layouts  9.01 us

profile of v1, /device:TPU:0, one launch (start us, length us, event | category | flops | bytes accessed | tf_op | source)
XLA Modules:
  0.0 61.7 jit_solution(6349993196506519991)
XLA Ops:
  1.9 0.8 %copy.16.ids_ref = s32[256,8]{1,0:T(8,128)S(1)} copy(s32[256,8]{0,1:T(8,128)} %param.23) | data formatting | bytes 16384 | tf_op args[9]
  2.7 0.8 %copy.17.gw_ref = f32[256,8]{1,0:T(8,128)S(1)} copy(f32[256,8]{0,1:T(8,128)} %param.24) | data formatting | bytes 16384 | tf_op args[10]
  3.6 0.0 copy-start
  3.6 1.2 %copy-done = bf16[128,4096]{1,0:T(8,128)(2,1)S(1)} copy-done((bf16[128,4096]{1,0:T(8,128)(2,1)S(1)}, bf16[128,4096]{1,0:T(8,128)(2,1)}, u32[]{:S(2)}) %copy-start) | copy-done | bytes 1048600
  4.8 0.0 copy-start.1
  4.8 0.9 %copy-done.1 = bf16[256,512]{1,0:T(8,128)(2,1)S(1)} copy-done((bf16[256,512]{1,0:T(8,128)(2,1)S(1)}, bf16[256,512]{1,0:T(8,128)(2,1)}, u32[]{:S(2)}) %copy-start.1) | copy-done | bytes 262168
  5.8 0.0 copy-start.2
  5.8 0.9 %copy-done.2 = bf16[256,512]{1,0:T(8,128)(2,1)S(1)} copy-done((bf16[256,512]{1,0:T(8,128)(2,1)S(1)}, bf16[256,512]{1,0:T(8,128)(2,1)}, u32[]{:S(2)}) %copy-start.2) | copy-done | bytes 262168
  6.7 0.0 copy-start.3
  6.7 0.9 %copy-done.3 = bf16[128,512]{1,0:T(8,128)(2,1)S(1)} copy-done((bf16[128,512]{1,0:T(8,128)(2,1)S(1)}, bf16[128,512]{1,0:T(8,128)(2,1)}, u32[]{:S(2)}) %copy-start.3) | copy-done | bytes 131096
  7.6 0.0 copy-start.4
  7.6 0.9 %copy-done.4 = bf16[128,512]{1,0:T(8,128)(2,1)S(1)} copy-done((bf16[128,512]{1,0:T(8,128)(2,1)S(1)}, bf16[128,512]{1,0:T(8,128)(2,1)}, u32[]{:S(2)}) %copy-start.4) | copy-done | bytes 131096
  8.5 0.0 copy-start.5
  8.5 0.7 %copy-done.5 = s32[256]{0:T(256)S(1)} copy-done((s32[256]{0:T(256)S(1)}, s32[256]{0:T(256)}, u32[]{:S(2)}) %copy-start.5) | copy-done | bytes 1048
  9.2 50.8 %shard_map.149 = (bf16[128,4096]{1,0:T(8,128)(2,1)S(1)}, bf16[256,1024]{1,0:T(8,128)(2,1)S(1)}) custom-call(bf16[128,4096]{1,0:T(8,128)(2,1)S(1)} %copy-done, bf16[128,512]{1,0:T(8,128)(2,1)S(1)} %copy-done.3, bf16[128,512]{1,0:T(8,128)(2,1)S(1)} %copy-done.4, bf16[256,512]{1,0:T(8,128)(2,1)S(1)} %copy-done.1, bf16[256,512]{1,0:T(8,128)(2,1)S(1)} %copy-done.2, ...), custom_call_target="tpu_custom_call" | custom-call | tf_op jit(solution)/shard_map/pallas_call | solution.py:497
  60.0 1.0 %copy.22 = bf16[128,4096]{1,0:T(8,128)(2,1)} copy(bf16[128,4096]{1,0:T(8,128)(2,1)S(1)} %get-tuple-element.4) | data formatting | bytes 2097152
  60.9 0.8 %copy.23 = bf16[256,1024]{1,0:T(8,128)(2,1)} copy(bf16[256,1024]{1,0:T(8,128)(2,1)S(1)} %get-tuple-element.5) | data formatting | bytes 1048576
Async XLA Ops:
  3.6 1.2 %copy-start = (bf16[128,4096]{1,0:T(8,128)(2,1)S(1)}, bf16[128,4096]{1,0:T(8,128)(2,1)}, u32[]{:S(2)}) copy-start(bf16[128,4096]{1,0:T(8,128)(2,1)} %q_ref.1) | copy-start | bytes 3145732
  4.8 0.9 %copy-start.1 = (bf16[256,512]{1,0:T(8,128)(2,1)S(1)}, bf16[256,512]{1,0:T(8,128)(2,1)}, u32[]{:S(2)}) copy-start(bf16[256,512]{1,0:T(8,128)(2,1)} %pk_ref.1) | copy-start | bytes 786436
  5.8 0.9 %copy-start.2 = (bf16[256,512]{1,0:T(8,128)(2,1)S(1)}, bf16[256,512]{1,0:T(8,128)(2,1)}, u32[]{:S(2)}) copy-start(bf16[256,512]{1,0:T(8,128)(2,1)} %pv_ref.1) | copy-start | bytes 786436
  6.7 0.9 %copy-start.3 = (bf16[128,512]{1,0:T(8,128)(2,1)S(1)}, bf16[128,512]{1,0:T(8,128)(2,1)}, u32[]{:S(2)}) copy-start(bf16[128,512]{1,0:T(8,128)(2,1)} %sk_ref.1) | copy-start | bytes 393220
  7.6 0.9 %copy-start.4 = (bf16[128,512]{1,0:T(8,128)(2,1)S(1)}, bf16[128,512]{1,0:T(8,128)(2,1)}, u32[]{:S(2)}) copy-start(bf16[128,512]{1,0:T(8,128)(2,1)} %sv_ref.1) | copy-start | bytes 393220
  8.5 0.7 %copy-start.5 = (s32[256]{0:T(256)S(1)}, s32[256]{0:T(256)}, u32[]{:S(2)}) copy-start(s32[256]{0:T(256)} %param.19) | copy-start | bytes 3076

commit v2 on v1

--- a/solution.py
+++ b/solution.py
@@ -18,13 +18,19 @@
 PAD = 16
 NEG = -1e30
 COEF = HD ** (-0.5) * math.log2(math.e)
-UNROLL = 4
+STACK = 2
+SLOTS = 2
 NT = (((1,), (1,)), ((), ()))
 MESH = pl.DeviceIdType.MESH
 F32 = jnp.float32
 BF16 = jnp.bfloat16
 
 
+def block_of(per_kv):
+    stack = math.gcd(STACK, per_kv)
+    return stack, math.gcd(SLOTS, per_kv // stack)
+
+
 def aligned(value, unit=128):
     return pl.multiple_of(value, unit)
 
@@ -36,15 +42,15 @@
 def kernel(
     ep,
     tp,
-    q_ref,
-    sk_ref,
-    sv_ref,
-    pk_ref,
-    pv_ref,
+    q_hbm,
+    sk_hbm,
+    sv_hbm,
+    pk_hbm,
+    pv_hbm,
     pg_ref,
     shots_ref,
     len_ref,
-    hid_ref,
+    hid_hbm,
     ids_ref,
     gw_ref,
     wg_hbm,
@@ -58,8 +64,15 @@
     ksuf,
     vsuf,
     sbias,
-    m_ref,
-    acc_ref,
+    q_ref,
+    sk_ref,
+    sv_ref,
+    pk_ref,
+    pv_ref,
+    hid_ref,
+    qs,
+    m_refs,
+    acc_refs,
     wg,
     wu,
     wd,
@@ -91,14 +104,15 @@
     r_sd,
     r_rv,
     w_sem,
+    i_sem,
 ):
     z = lax.axis_index("ep")
     x = lax.axis_index("tp")
     c = lax.axis_index("pp")
     me = z * 2 + c
     other = 1 - c
-    rows = pk_ref.shape[0]
-    heads = q_ref.shape[1] // HD
+    rows = pk_hbm.shape[0]
+    heads = q_hbm.shape[1] // HD
     group = HEADS // KVH
     kvh = max(1, heads // group)
     per_kv = min(heads, group)
@@ -115,6 +129,24 @@
     for o in range(1, tp):
         pl.semaphore_signal(barrier, inc=1, device_id={"tp": lax.rem(x + o, tp)}, device_id_type=MESH)
 
+    first = aligned(x * heads // group * HD)
+    own_columns = pl.ds(first, kvw)
+    input_copies = [
+        pltpu.make_async_copy(src, dst, i_sem.at[i])
+        for i, (src, dst) in enumerate(
+            (
+                (pk_hbm.at[:, own_columns], pk_ref),
+                (pv_hbm.at[:, own_columns], pv_ref),
+                (hid_hbm.at[:, pl.ds(aligned(x * part), part)], hid_ref.at[0]),
+                (hid_hbm.at[:, pl.ds(aligned(half + x * part), part)], hid_ref.at[1]),
+                (sk_hbm.at[:, own_columns], sk_ref),
+                (sv_hbm.at[:, own_columns], sv_ref),
+                (q_hbm, q_ref),
+            )
+        )
+    ]
+    for copy in input_copies:
+        copy.start()
     weight_copies = [
         pltpu.make_async_copy(src.at[0], dst, w_sem.at[i])
         for i, (src, dst) in enumerate(((wg_hbm, wg), (wu_hbm, wu), (wd_hbm, wd)))
@@ -122,43 +154,44 @@
     for copy in weight_copies:
         copy.start()
 
-    first = aligned(x * heads // group * HD)
-    kv[z, c, 0:rows, :] = pk_ref[:, pl.ds(first, kvw)]
-    kv[z, c, rows : 2 * rows, :] = pv_ref[:, pl.ds(first, kvw)]
+    for copy in input_copies[0:2]:
+        copy.wait()
+    kv[z, c, 0:rows, :] = pk_ref[...]
+    kv[z, c, rows : 2 * rows, :] = pv_ref[...]
     ids_row = pg_ref[...].astype(F32)
     if rows < kvw:
         ids_row = jnp.concatenate([ids_row, jnp.zeros((1, kvw - rows), F32)], axis=1)
     kv[z, c, 2 * rows : 2 * rows + 16, :] = jnp.broadcast_to(ids_row, (16, kvw)).astype(BF16)
 
-    lane = lax.broadcasted_iota(jnp.int32, (SUFFIX, lanes), 1)
-    expert_of = lax.shift_right_logical(lane, 4)
-    slot_of = lane & (PAD - 1)
-    usable = (slot_of < CAP) & (lane < ep * PAD)
-    below = (
-        lax.broadcasted_iota(jnp.int32, (SUFFIX, SUFFIX), 1)
-        < lax.broadcasted_iota(jnp.int32, (SUFFIX, SUFFIX), 0)
+    line = lax.broadcasted_iota(jnp.int32, (lanes, SUFFIX), 0)
+    expert_of = lax.shift_right_logical(line, 4)
+    slot_of = line & (PAD - 1)
+    usable = (slot_of < CAP) & (line < ep * PAD)
+    earlier = (
+        lax.broadcasted_iota(jnp.int32, (SUFFIX, SUFFIX), 0)
+        < lax.broadcasted_iota(jnp.int32, (SUFFIX, SUFFIX), 1)
     )
-    below = jnp.where(below, 1.0, 0.0).astype(BF16)
+    earlier = jnp.where(earlier, 1.0, 0.0).astype(BF16)
     tables = []
     for b in range(2):
-        taken = jnp.zeros((SUFFIX, lanes), F32)
-        share = jnp.zeros((SUFFIX, lanes), F32)
+        taken = jnp.zeros((lanes, SUFFIX), F32)
+        share = jnp.zeros((lanes, SUFFIX), F32)
         for k in range(TOP):
-            named = ids_ref[b * SUFFIX : (b + 1) * SUFFIX, k : k + 1] == expert_of
+            named = ids_ref[k : k + 1, b * SUFFIX : (b + 1) * SUFFIX] == expert_of
             taken = jnp.where(named, 1.0, taken)
-            share = share + jnp.where(named, gw_ref[b * SUFFIX : (b + 1) * SUFFIX, k : k + 1], 0.0)
-        slot = jnp.dot(below, taken.astype(BF16), preferred_element_type=F32)
+            share = share + jnp.where(named, gw_ref[k : k + 1, b * SUFFIX : (b + 1) * SUFFIX], 0.0)
+        slot = jnp.dot(taken.astype(BF16), earlier, preferred_element_type=F32)
         hit = (taken > 0.0) & usable & (slot == slot_of.astype(F32))
         tables.append(jnp.where(hit, 1.0, 0.0))
-        weight = jnp.where(hit, share, 0.0)
-        high = weight.astype(BF16)
-        whi[b] = high
-        wlo[b] = (weight - high.astype(F32)).astype(BF16)
-    own_table = jnp.where(c == 0, tables[0], tables[1])
-    pick = own_table.T.astype(BF16)
+        weight = jnp.where(hit, share, 0.0).T
+        upper = weight.astype(BF16)
+        whi[b] = upper
+        wlo[b] = (weight - upper.astype(F32)).astype(BF16)
+    pick = jnp.where(c == 0, tables[0], tables[1]).astype(BF16)
+    for copy in input_copies[2:4]:
+        copy.wait()
     for p in range(2):
-        columns = aligned(p * half + x * part)
-        chosen = jnp.dot(pick, hid_ref[:, pl.ds(columns, part)], preferred_element_type=F32).astype(BF16)
+        chosen = jnp.dot(pick, hid_ref[p], preferred_element_type=F32).astype(BF16)
         for e in range(ep):
             dsend[e * 2 + p] = chosen[e * PAD : (e + 1) * PAD]
     xbuf[x, me] = dsend[me]
@@ -253,30 +286,37 @@
 
             pair_copy(high, c).start()
 
+    for copy in input_copies[4:]:
+        copy.wait()
+    for h in range(heads):
+        qs[h] = q_ref[:, h * HD : (h + 1) * HD]
     length = len_ref[0]
     shots = shots_ref[0].astype(F32)
     row_id = lax.broadcasted_iota(jnp.int32, (SUFFIX, SUFFIX), 0)
     col_id = lax.broadcasted_iota(jnp.int32, (SUFFIX, SUFFIX), 1)
     sbias[...] = jnp.where((col_id <= row_id) & (col_id < length), 0.0, NEG)
     for g in range(kvh):
-        ksuf[g] = sk_ref[:, pl.ds(aligned(first + g * HD), HD)]
-        vsuf[g, :, 0:HD] = sv_ref[:, pl.ds(aligned(first + g * HD), HD)]
+        ksuf[g] = sk_ref[:, g * HD : (g + 1) * HD]
+        vsuf[g, :, 0:HD] = sv_ref[:, g * HD : (g + 1) * HD]
         vsuf[g, :, HD:] = jnp.ones((SUFFIX, HD), BF16)
         vscr[g, :, HD:] = jnp.ones((2 * rows, HD), BF16)
 
-    unroll = math.gcd(UNROLL, per_kv)
+    stack, slots = block_of(per_kv)
+    step = stack * slots
+    high = stack * SUFFIX
 
     def own_keys(g):
-        @pl.loop(0, per_kv // unroll)
+        @pl.loop(0, per_kv // step)
         def _(i):
-            for u in range(unroll):
-                h = g * per_kv + i * unroll + u
-                query = q_ref[:, pl.ds(aligned(h * HD), HD)]
-                s = lax.dot_general(query, ksuf[g], NT, preferred_element_type=F32) + sbias[...]
-                top = jnp.broadcast_to(jnp.max(s, axis=1, keepdims=True), (SUFFIX, HD))
+            for u in range(slots):
+                b = g * (per_kv // step) + i
+                query = qs[pl.ds(b * step + u * stack, stack)].reshape(high, HD)
+                s = lax.dot_general(query, ksuf[g], NT, preferred_element_type=F32)
+                s = (s.reshape(stack, SUFFIX, SUFFIX) + sbias[...]).reshape(high, SUFFIX)
+                top = jnp.broadcast_to(jnp.max(s, axis=1, keepdims=True), (high, HD))
                 weight = jnp.exp2((s - top) * COEF).astype(BF16)
-                m_ref[h] = top
-                acc_ref[h] = jnp.dot(weight, vsuf[g], preferred_element_type=F32)
+                m_refs[u][b] = top
+                acc_refs[u][b] = jnp.dot(weight, vsuf[g], preferred_element_type=F32)
 
     def load_chunk(chunk):
         for core in range(2):
@@ -292,25 +332,28 @@
         return jnp.where(groups < shots, 0.0, NEG)
 
     def prefix_keys(g, bias, last):
-        @pl.loop(0, per_kv // unroll)
+        @pl.loop(0, per_kv // step)
         def _(i):
-            for u in range(unroll):
-                h = g * per_kv + i * unroll + u
-                columns = pl.ds(aligned(h * HD), HD)
-                s = lax.dot_general(q_ref[:, columns], kscr[g], NT, preferred_element_type=F32) + bias
-                before = m_ref[h]
+            b = g * (per_kv // step) + i
+            for u in range(slots):
+                query = qs[pl.ds(b * step + u * stack, stack)].reshape(high, HD)
+                s = lax.dot_general(query, kscr[g], NT, preferred_element_type=F32) + bias
+                before = m_refs[u][b]
                 top = jnp.maximum(before, jnp.max(s, axis=1, keepdims=True))
                 weight = jnp.exp2((s - wide(top, 2 * rows)) * COEF).astype(BF16)
                 factor = jnp.exp2((before - top) * COEF)
-                total = acc_ref[h] * wide(factor, 2 * HD) + jnp.dot(
+                total = acc_refs[u][b] * wide(factor, 2 * HD) + jnp.dot(
                     weight, vscr[g], preferred_element_type=F32
                 )
                 if last:
                     mean = total[:, 0:HD] / total[:, HD:]
-                    ctx_ref[:, columns] = jnp.where(row_id < length, mean, 0.0).astype(BF16)
+                    for t in range(stack):
+                        block = mean[t * SUFFIX : (t + 1) * SUFFIX]
+                        columns = pl.ds(aligned((b * step + u * stack + t) * HD), HD)
+                        ctx_ref[:, columns] = jnp.where(row_id < length, block, 0.0).astype(BF16)
                 else:
-                    m_ref[h] = top
-                    acc_ref[h] = total
+                    m_refs[u][b] = top
+                    acc_refs[u][b] = total
 
     def share_copy(o, block):
         return pltpu.make_async_remote_copy(
@@ -490,6 +533,8 @@
     lanes = -(-ep * PAD // 128) * 128
     tokens = 2 * ep * PAD
     assert tok_rows == SUFFIX and rows <= kvw
+    stack, slots = block_of(min(heads, HEADS // KVH))
+    step = stack * slots
     vmem = pl.BlockSpec(memory_space=pltpu.VMEM)
     smem = pl.BlockSpec(memory_space=pltpu.SMEM)
     hbm = pl.BlockSpec(memory_space=pl.ANY)
@@ -500,7 +545,7 @@
             jax.ShapeDtypeStruct((tok_rows, q_width), BF16),
             jax.ShapeDtypeStruct((2 * tok_rows, part), BF16),
         ),
-        in_specs=[vmem] * 6 + [smem] * 2 + [vmem] * 3 + [hbm] * 3,
+        in_specs=[hbm] * 5 + [vmem] + [smem] * 2 + [hbm] + [vmem] * 2 + [hbm] * 3,
         out_specs=(vmem, vmem),
         scratch_shapes=[
             pltpu.VMEM((ep, 2, 2 * rows + 16, kvw), BF16),
@@ -509,8 +554,15 @@
             pltpu.VMEM((kvh, SUFFIX, HD), BF16),
             pltpu.VMEM((kvh, SUFFIX, 2 * HD), BF16),
             pltpu.VMEM((SUFFIX, SUFFIX), F32),
-            pltpu.VMEM((heads, SUFFIX, HD), F32),
-            pltpu.VMEM((heads, SUFFIX, 2 * HD), F32),
+            pltpu.VMEM((tok_rows, q_width), BF16),
+            pltpu.VMEM((tok_rows, kvw), BF16),
+            pltpu.VMEM((tok_rows, kvw), BF16),
+            pltpu.VMEM((rows, kvw), BF16),
+            pltpu.VMEM((rows, kvw), BF16),
+            pltpu.VMEM((2, tok_rows, part), BF16),
+            pltpu.VMEM((heads, SUFFIX, HD), BF16),
+            [pltpu.VMEM((heads // step, stack * SUFFIX, HD), F32)] * slots,
+            [pltpu.VMEM((heads // step, stack * SUFFIX, 2 * HD), F32)] * slots,
             pltpu.VMEM((half, units), BF16),
             pltpu.VMEM((half, units), BF16),
             pltpu.VMEM((units, half), BF16),
@@ -542,9 +594,10 @@
             dma((ep,)),
             dma((ep,)),
             dma((3,)),
+            dma((7,)),
         ],
         compiler_params=pltpu.CompilerParams(
-            collective_id=0, has_side_effects=True, vmem_limit_bytes=50 * 1024 * 1024
+            collective_id=0, has_side_effects=True, vmem_limit_bytes=56 * 1024 * 1024
         ),
     )(
         queries,
@@ -556,8 +609,8 @@
         shot_counts,
         lengths,
         hidden,
-        expert_ids,
-        gate_weights,
+        expert_ids.T,
+        gate_weights.T,
         gate_proj,
         up_proj,
         down_proj,

time: 62.1 us -> 57.2 us (0.921)
  local copies, waits for them, and re-layouts: 9.01 us -> 4.16 us
    unnamed x16 -> x2, local copies, waits for them, and re-layouts: 9.01 us -> 4.16 us
where the time goes in v2:
time: 57.2 us; the launch traced here: 56.9 us
  Pallas kernels  50.8 us (89%)
  local copies, waits for them, and re-layouts  4.16 us (7%)
  between operations  1.93 us (3%)
    pallas_call x1, Pallas kernels, shards(): pl.pallas_call(functools.partial(kernel, ep, tp), out_shape=(jax.ShapeDty...  50.8 us
    unnamed x2, local copies, waits for them, and re-layouts  4.16 us

profile of v2, /device:TPU:0, one launch (start us, length us, event | category | flops | bytes accessed | tf_op | source)
XLA Modules:
  0.0 56.9 jit_solution(17964154056497277719)
XLA Ops:
  1.9 50.8 %shard_map.149 = (bf16[128,4096]{1,0:T(8,128)(2,1)}, bf16[256,1024]{1,0:T(8,128)(2,1)}) custom-call(bf16[128,4096]{1,0:T(8,128)(2,1)} %q_hbm.1, bf16[128,512]{1,0:T(8,128)(2,1)} %sk_hbm.1, bf16[128,512]{1,0:T(8,128)(2,1)} %sv_hbm.1, bf16[256,512]{1,0:T(8,128)(2,1)} %pk_hbm.1, bf16[256,512]{1,0:T(8,128)(2,1)} %pv_hbm.1, s32[1,256]{1,0:T(1,128)} %bitcast.5, ...), custom_call_target="tpu_custom_call" | custom-call | tf_op jit(solution)/shard_map/pallas_call | solution.py:542
  52.8 2.3 %copy.20 = bf16[128,4096]{1,0:T(8,128)(2,1)} copy(bf16[128,4096]{1,0:T(8,128)(2,1)} %get-tuple-element.4) | data formatting | bytes 2097152
  55.1 1.9 %copy.21 = bf16[256,1024]{1,0:T(8,128)(2,1)} copy(bf16[256,1024]{1,0:T(8,128)(2,1)} %get-tuple-element.5) | data formatting | bytes 1048576
